TPU v7x, 512 devices: a whole 4x4x16 slice. The times are simulated.
512 devices in a mesh: resp: 64 (over x, z_lo, core), tp: 8 (over y, z_hi).
Axes of the slice: x: 4, y: 4, z: 16 (z_hi: 2, z_lo: 8; z = z_hi * 8 + z_lo), core: 2. Of those that a mesh axis runs over, the one named last changes fastest.
Arguments:
- queries: bfloat16 [16384, 8192], P(('resp', 'tp')), may hold values from -6 to 6
- keys: bfloat16 [16384, 1024], P(('resp', 'tp')), may hold values from -6 to 6
- values: bfloat16 [16384, 1024], P(('resp', 'tp')), may hold values from -6 to 6
- out_grad: bfloat16 [16384, 8192], P(('resp', 'tp')), may hold values from -6 to 6
- prefix_keys: bfloat16 [4096, 1024], P('resp', 'tp'), may hold values from -6 to 6
- prefix_values: bfloat16 [4096, 1024], P('resp', 'tp'), may hold values from -6 to 6
- lengths: int32 [128], P('resp'), may hold values from 1 to 128, 10240 in all
- prompt_of: int32 [128], P('resp'), may hold values from 0 to 7, as said below
Outputs:
- grad_queries: bfloat16 [16384, 8192], P(('resp', 'tp'))
- grad_keys: bfloat16 [16384, 1024], P(('resp', 'tp'))
- grad_values: bfloat16 [16384, 1024], P(('resp', 'tp'))
- grad_prefix_keys: bfloat16 [4096, 1024], P('resp', 'tp')
- grad_prefix_values: bfloat16 [4096, 1024], P('resp', 'tp')
Inputs may be any that keep to these rules, and one draw needn't show every extreme that they name: `prompt_of`: every prompt is the prompt of exactly 16 responses. `lengths`: some response has all 128 slots live.
All inputs are finite; a program needn't handle non-finite values. No bound on the sum of `lengths` on one device may be relied on, other than what follows from the above.
Results may differ from a plain program's by a relative error of at most 0.011.
Values may be sent and summed in bfloat16 or wider, within the bound.
A program may use at most 64 MiB of HBM per device.

v0:
```python
import math

import jax
import jax.numpy as jnp
from jax import lax
from jax.sharding import PartitionSpec as P

HD = 128
RCAP = 128
PLEN = 512


def body(queries, keys, values, out_grad, prefix_keys, prefix_values, lengths, prompt_of):
    scale = 1.0 / math.sqrt(HD)
    f32 = jnp.float32
    bf16 = jnp.bfloat16
    q_heads, k_heads, v_heads, g_heads = (
        lax.all_to_all(queries, "tp", split_axis=1, concat_axis=0, tiled=True),
        lax.all_to_all(keys, "tp", split_axis=1, concat_axis=0, tiled=True),
        lax.all_to_all(values, "tp", split_axis=1, concat_axis=0, tiled=True),
        lax.all_to_all(out_grad, "tp", split_axis=1, concat_axis=0, tiled=True),
    )
    whole_keys, whole_values = (
        lax.all_gather(prefix_keys, "resp", axis=0, tiled=True),
        lax.all_gather(prefix_values, "resp", axis=0, tiled=True),
    )
    groups = k_heads.shape[1] // HD
    repeat = q_heads.shape[1] // k_heads.shape[1]
    slots = lengths.shape[0]
    positions = jnp.arange(RCAP, dtype=jnp.int32)
    causal = positions[None, :] <= positions[:, None]
    saved = []
    for slot in range(slots):
        low = slot * RCAP
        q_rows = q_heads[low : low + RCAP].reshape(RCAP, groups, repeat, HD)
        k_rows = k_heads[low : low + RCAP].reshape(RCAP, groups, HD)
        v_rows = v_heads[low : low + RCAP].reshape(RCAP, groups, HD)
        first = prompt_of[slot] * PLEN
        p_keys = lax.dynamic_slice_in_dim(whole_keys, first, PLEN, 0).reshape(PLEN, groups, HD)
        p_vals = lax.dynamic_slice_in_dim(whole_values, first, PLEN, 0).reshape(PLEN, groups, HD)
        s_pre = jnp.einsum("ighd,jgd->ghij", q_rows, p_keys, preferred_element_type=f32) * scale
        s_self = jnp.einsum("ighd,jgd->ghij", q_rows, k_rows, preferred_element_type=f32) * scale
        s_self = jnp.where(causal, s_self, -jnp.inf)
        top = jnp.maximum(jnp.max(s_pre, -1), jnp.max(s_self, -1))
        e_pre = jnp.exp(s_pre - top[..., None])
        e_self = jnp.exp(s_self - top[..., None])
        total = jnp.sum(e_pre, -1) + jnp.sum(e_self, -1)
        p_pre = e_pre / total[..., None]
        p_self = e_self / total[..., None]
        b_pre = p_pre.astype(bf16)
        b_self = p_self.astype(bf16)
        attn = jnp.einsum("ghij,jgd->ighd", b_pre, p_vals, preferred_element_type=f32) + jnp.einsum(
            "ghij,jgd->ighd", b_self, v_rows, preferred_element_type=f32
        )
        saved.append(
            (q_rows, k_rows, v_rows, p_keys, p_vals, p_pre, p_self, b_pre, b_self, attn, first)
        )
    term = jnp.zeros((whole_keys.shape[0], 2 * groups * HD), f32)
    dq_list, dk_list, dv_list = ([], [], [])
    for slot in range(slots):
        cotangent_low = slot * RCAP
        live = positions < lengths[slot]
        rows = g_heads[cotangent_low : cotangent_low + RCAP]
        rows = jnp.where(live[:, None], rows, jnp.zeros_like(rows))
        cotangent_grads = rows.reshape(RCAP, groups, repeat, HD)
        cotangent_attn = saved[slot][9]
        cotangent_delta = jnp.transpose(
            jnp.sum(cotangent_grads.astype(f32) * cotangent_attn, -1), (1, 2, 0)
        )
        (
            prefix_q_rows,
            prefix_k_rows,
            prefix_v_rows,
            prefix_p_keys,
            prefix_p_vals,
            prefix_p_pre,
            prefix_p_self,
            prefix_b_pre,
            prefix_b_self,
            prefix_attn,
            prefix_first,
        ) = saved[slot]
        dp_pre = jnp.einsum(
            "ighd,jgd->ghij", cotangent_grads, prefix_p_vals, preferred_element_type=f32
        )
        ds_pre = (prefix_p_pre * (dp_pre - cotangent_delta[..., None])).astype(bf16)
        prefix_dq_pre = jnp.einsum(
            "ghij,jgd->ighd", ds_pre, prefix_p_keys, preferred_element_type=f32
        )
        dpk = (
            jnp.einsum("ghij,ighd->jgd", ds_pre, prefix_q_rows, preferred_element_type=f32) * scale
        )
        dpv = jnp.einsum(
            "ghij,ighd->jgd", prefix_b_pre, cotangent_grads, preferred_element_type=f32
        )
        prefix_block = jnp.concatenate(
            [dpk.reshape(PLEN, groups * HD), dpv.reshape(PLEN, groups * HD)], 1
        )
        first = prefix_first
        current = lax.dynamic_slice_in_dim(term, first, PLEN, 0)
        term = lax.dynamic_update_slice_in_dim(term, current + prefix_block, first, 0)
        (
            self_q_rows,
            self_k_rows,
            self_v_rows,
            self_p_keys,
            self_p_vals,
            self_p_pre,
            self_p_self,
            self_b_pre,
            self_b_self,
            self_attn,
            self_first,
        ) = saved[slot]
        dp_self = jnp.einsum(
            "ighd,jgd->ghij", cotangent_grads, self_v_rows, preferred_element_type=f32
        )
        ds_self = (self_p_self * (dp_self - cotangent_delta[..., None])).astype(bf16)
        dq_self = jnp.einsum("ghij,jgd->ighd", ds_self, self_k_rows, preferred_element_type=f32)
        dq = ((prefix_dq_pre + dq_self) * scale).astype(bf16).reshape(RCAP, groups * repeat * HD)
        dk = (
            jnp.einsum("ghij,ighd->jgd", ds_self, self_q_rows, preferred_element_type=f32) * scale
        ).astype(bf16)
        dv = jnp.einsum(
            "ghij,ighd->jgd", self_b_self, cotangent_grads, preferred_element_type=f32
        ).astype(bf16)
        dq, dk, dv = (dq, dk.reshape(RCAP, groups * HD), dv.reshape(RCAP, groups * HD))
        dq_list.append(dq)
        dk_list.append(dk)
        dv_list.append(dv)
    shares = lax.psum_scatter(term, "resp", scatter_dimension=0, tiled=True)
    dq_all = jnp.concatenate(dq_list, 0)
    dk_all = jnp.concatenate(dk_list, 0)
    dv_all = jnp.concatenate(dv_list, 0)
    grad_queries, grad_keys, grad_values = (
        lax.all_to_all(dq_all, "tp", split_axis=0, concat_axis=1, tiled=True),
        lax.all_to_all(dk_all, "tp", split_axis=0, concat_axis=1, tiled=True),
        lax.all_to_all(dv_all, "tp", split_axis=0, concat_axis=1, tiled=True),
    )
    feature_width = groups * HD
    grad_prefix_keys = shares[:, :feature_width].astype(bf16)
    grad_prefix_values = shares[:, feature_width:].astype(bf16)
    return (grad_queries, grad_keys, grad_values, grad_prefix_keys, grad_prefix_values)


def solution(mesh):
    in_specs = (
        P(("resp", "tp"), None),
        P(("resp", "tp"), None),
        P(("resp", "tp"), None),
        P(("resp", "tp"), None),
        P("resp", "tp"),
        P("resp", "tp"),
        P("resp"),
        P("resp"),
    )
    out_specs = (
        P(("resp", "tp"), None),
        P(("resp", "tp"), None),
        P(("resp", "tp"), None),
        P("resp", "tp"),
        P("resp", "tp"),
    )
    return jax.shard_map(body, mesh=mesh, in_specs=in_specs, out_specs=out_specs, check_vma=False)
```

profile of v0, /device:TPU:8, one launch (start us, length us, event | category | flops | bytes accessed | tf_op | source)
XLA Modules:
  0.0 803.5 jit_solution(7031693314855086843)
XLA Ops:
  8.7 18.2 %all-to-all-start.1 = ((bf16[32,8,128]{2,0,1:T(8,128)(2,1)}), bf16[32,8,128]{2,0,1:T(8,128)(2,1)S(1)}, u32[]{:S(2)}, u32[]{:S(2)}) async-start(bf16[32,8,128]{2,0,1:T(8,128)(2,1)} %copy_bitcast_fusion.5), calls=%async_computation.1 | async-start | bytes 131072 | tf_op jit(solution)/shard_map/all_to_all | solution.py:19
  28.3 12.1 %all-to-all-done.1 = bf16[32,8,128]{2,0,1:T(8,128)(2,1)S(1)} async-done(((bf16[32,8,128]{2,0,1:T(8,128)(2,1)}), bf16[32,8,128]{2,0,1:T(8,128)(2,1)S(1)}, u32[]{:S(2)}, u32[]{:S(2)}) %all-to-all-start.1) | async-done | bytes 65568 | tf_op jit(solution)/shard_map/all_to_all | solution.py:19
  40.4 4.7 all-to-all-start.3
  45.1 1.9 copy.255
  47.1 11.7 %all-to-all-done.3 = bf16[32,8,128]{2,0,1:T(8,128)(2,1)S(1)} async-done(((bf16[32,8,128]{2,0,1:T(8,128)(2,1)}), bf16[32,8,128]{2,0,1:T(8,128)(2,1)S(1)}, u32[]{:S(2)}, u32[]{:S(2)}) %all-to-all-start.3) | async-done | bytes 65568 | tf_op jit(solution)/shard_map/all_to_all | solution.py:20
  58.8 4.9 all-to-all-start
  65.2 25.4 %all-to-all-done = bf16[32,8,1024]{2,0,1:T(8,128)(2,1)S(1)} async-done(((bf16[32,8,1024]{2,0,1:T(8,128)(2,1)}), bf16[32,8,1024]{2,0,1:T(8,128)(2,1)S(1)}, u32[]{:S(2)}, u32[]{:S(2)}) %all-to-all-start) | async-done | bytes 524320 | tf_op jit(solution)/shard_map/all_to_all | solution.py:18
  90.6 3.4 all-to-all-start.2
  101.3 22.6 %all-to-all-done.2 = bf16[32,8,1024]{2,0,1:T(8,128)(2,1)S(1)} async-done(((bf16[32,8,1024]{2,0,1:T(8,128)(2,1)}), bf16[32,8,1024]{2,0,1:T(8,128)(2,1)S(1)}, u32[]{:S(2)}, u32[]{:S(2)}) %all-to-all-start.2) | async-done | bytes 524320 | tf_op jit(solution)/shard_map/all_to_all | solution.py:21
  130.5 74.6 %all-gather.3.cloned.1.call-done = bf16[4096,128]{1,0:T(8,128)(2,1)} async-done(((bf16[64,128]{1,0:T(8,128)(2,1)}), bf16[4096,128]{1,0:T(8,128)(2,1)}) %all-gather.3.cloned.1.call-update) | async-done | bytes 1048592 | tf_op jit(solution)/shard_map/all_gather | solution.py:24
  207.4 1.7 copy.192
  214.6 106.2 %all-gather.5.cloned.1.call-done = bf16[4096,128]{1,0:T(8,128)(2,1)} async-done(((bf16[64,128]{1,0:T(8,128)(2,1)}), bf16[4096,128]{1,0:T(8,128)(2,1)}) %all-gather.5.cloned.1.call-update) | async-done | bytes 1048592 | tf_op jit(solution)/shard_map/all_gather | solution.py:25
  322.3 1.7 fusion.11
  326.2 1.7 copy.189
  333.9 2.5 broadcast_in_dim.60
  337.3 2.0 fusion.44
  339.3 5.6 copy.223
  349.1 10.8 %all-to-all-start.6 = ((bf16[8,32,128]{2,1,0:T(8,128)(2,1)}), bf16[8,32,128]{2,1,0:T(8,128)(2,1)}, u32[]{:S(2)}, u32[]{:S(2)}) async-start(bf16[8,32,128]{2,1,0:T(8,128)(2,1)} %bitcast.94), calls=%async_computation.6 | async-start | bytes 131072 | tf_op jit(solution)/shard_map/all_to_all | solution.py:138
  365.4 8.5 %all-to-all-done.6 = bf16[8,32,128]{2,1,0:T(8,128)(2,1)} async-done(((bf16[8,32,128]{2,1,0:T(8,128)(2,1)}), bf16[8,32,128]{2,1,0:T(8,128)(2,1)}, u32[]{:S(2)}, u32[]{:S(2)}) %all-to-all-start.6) | async-done | bytes 65568 | tf_op jit(solution)/shard_map/all_to_all | solution.py:138
  373.9 5.9 all-to-all-start.5
  382.2 11.4 %all-to-all-done.5 = bf16[8,32,128]{2,1,0:T(8,128)(2,1)S(1)} async-done(((bf16[8,32,128]{2,1,0:T(8,128)(2,1)}), bf16[8,32,128]{2,1,0:T(8,128)(2,1)S(1)}, u32[]{:S(2)}, u32[]{:S(2)}) %all-to-all-start.5) | async-done | bytes 65568 | tf_op jit(solution)/shard_map/all_to_all | solution.py:137
  393.6 4.9 all-to-all-start.4
  400.7 15.0 %all-to-all-done.4 = bf16[8,32,1024]{2,1,0:T(8,128)(2,1)S(1)} async-done(((bf16[8,32,1024]{2,1,0:T(8,128)(2,1)}), bf16[8,32,1024]{2,1,0:T(8,128)(2,1)S(1)}, u32[]{:S(2)}, u32[]{:S(2)}) %all-to-all-start.4) | async-done | bytes 524320 | tf_op jit(solution)/shard_map/all_to_all | solution.py:136
  416.5 378.1 %reduce-scatter.4.cloned.1.call-done = f32[64,256]{1,0:T(8,128)} async-done(((f32[4096,256]{1,0:T(8,128)}), f32[64,256]{1,0:T(8,128)}) %reduce-scatter.4.cloned.1.call-update) | async-done | bytes 65552
  (145 shorter events, 52.2 us)
Async XLA Ops:
  7.2 57.2 %copy-start.23 = (bf16[32,8192]{1,0:T(8,128)(2,1)S(1)}, bf16[32,8192]{1,0:T(8,128)(2,1)}, u32[]{:S(2)}) copy-start(bf16[32,8192]{1,0:T(8,128)(2,1)} %param.11) | copy-start | bytes 1572868
  8.7 31.8 %all-to-all-start.1 = ((bf16[32,8,128]{2,0,1:T(8,128)(2,1)}), bf16[32,8,128]{2,0,1:T(8,128)(2,1)S(1)}, u32[]{:S(2)}, u32[]{:S(2)}) async-start(bf16[32,8,128]{2,0,1:T(8,128)(2,1)} %copy_bitcast_fusion.5), calls=%async_computation.1 | async-start | bytes 131072 | tf_op jit(solution)/shard_map/all_to_all | solution.py:19
  40.4 18.4 %all-to-all-start.3 = ((bf16[32,8,128]{2,0,1:T(8,128)(2,1)}), bf16[32,8,128]{2,0,1:T(8,128)(2,1)S(1)}, u32[]{:S(2)}, u32[]{:S(2)}) async-start(bf16[32,8,128]{2,0,1:T(8,128)(2,1)} %copy_bitcast_fusion.4), calls=%async_computation.3 | async-start | bytes 131072 | tf_op jit(solution)/shard_map/all_to_all | solution.py:20
  45.1 49.7 %copy-start.30 = (s32[2]{0:T(128)S(1)}, s32[2]{0:T(128)}, u32[]{:S(2)}) copy-start(s32[2]{0:T(128)} %param.15) | copy-start | bytes 28
  45.1 51.6 %copy-start.31 = (s32[2]{0:T(128)S(1)}, s32[2]{0:T(128)}, u32[]{:S(2)}) copy-start(s32[2]{0:T(128)} %param.14) | copy-start | bytes 28
  58.8 31.8 %all-to-all-start = ((bf16[32,8,1024]{2,0,1:T(8,128)(2,1)}), bf16[32,8,1024]{2,0,1:T(8,128)(2,1)S(1)}, u32[]{:S(2)}, u32[]{:S(2)}) async-start(bf16[32,8,1024]{2,0,1:T(8,128)(2,1)} %bitcast.362), calls=%async_computation | async-start | bytes 1048576 | tf_op jit(solution)/shard_map/all_to_all | solution.py:18
  63.6 141.5 %all-gather.3.cloned.1.call-start = ((), (), s32[]{:S(2)}) async-start(), calls=%async_computation.8 | async-start | bytes 1064960 | tf_op jit(solution)/shard_map/all_gather | solution.py:24
  90.6 33.3 %all-to-all-start.2 = ((bf16[32,8,1024]{2,0,1:T(8,128)(2,1)}), bf16[32,8,1024]{2,0,1:T(8,128)(2,1)S(1)}, u32[]{:S(2)}, u32[]{:S(2)}) async-start(bf16[32,8,1024]{2,0,1:T(8,128)(2,1)} %bitcast.361), calls=%async_computation.2 | async-start | bytes 1048576 | tf_op jit(solution)/shard_map/all_to_all | solution.py:21
  94.0 226.7 %all-gather.5.cloned.1.call-start = ((), (), s32[]{:S(2)}) async-start(), calls=%async_computation.9 | async-start | bytes 1064960 | tf_op jit(solution)/shard_map/all_gather | solution.py:25
  94.8 699.8 %reduce-scatter.4.cloned.1.call-start = ((), (), s32[]{:S(2)}) async-start(), calls=%async_computation.10 | async-start | bytes 4259840
  98.0 27.6 %copy-start.28 = (pred[128]{0:T(512)(128)(4,1)}, pred[128]{0:T(512)(128)(4,1)S(1)}, u32[]{:S(2)}) copy-start(pred[128]{0:T(512)(128)(4,1)S(1)} %iota_compare_fusion.2) | copy-start | bytes 388
  98.6 28.8 %copy-start.29 = (pred[128]{0:T(512)(128)(4,1)}, pred[128]{0:T(512)(128)(4,1)S(1)}, u32[]{:S(2)}) copy-start(pred[128]{0:T(512)(128)(4,1)S(1)} %iota_compare_fusion.1) | copy-start | bytes 388
  101.2 103.9 %copy-start.4 = (bf16[128,8,128]{0,2,1:T(8,128)(2,1)}, bf16[128,8,128]{0,2,1:T(8,128)(2,1)S(1)}, u32[]{:S(2)}) copy-start(bf16[128,8,128]{0,2,1:T(8,128)(2,1)S(1)} %copy.191) | copy-start | bytes 786436
  129.5 77.4 %copy-start.9 = (f32[1,8,128,128]{2,3,1,0:T(8,128)}, f32[1,8,128,128]{2,3,1,0:T(8,128)S(1)}, u32[]{:S(2)}) copy-start(f32[1,8,128,128]{2,3,1,0:T(8,128)S(1)} %get-tuple-element.44) | copy-start | bytes 1572868
  322.3 2.8 copy-start.5
  326.2 4.3 copy-start.2
  327.9 2.6 copy-start.24
  333.9 3.4 copy-start.22
  345.8 14.1 %copy-start.11 = (f32[1,8,128,128]{2,3,1,0:T(8,128)S(1)}, f32[1,8,128,128]{2,3,1,0:T(8,128)}, u32[]{:S(2)}) copy-start(f32[1,8,128,128]{2,3,1,0:T(8,128)} %copy-done.9) | copy-start | bytes 1572868
  346.9 14.3 %copy-start.8 = (f32[1,8,128,128]{2,3,1,0:T(8,128)S(1)}, f32[1,8,128,128]{2,3,1,0:T(8,128)}, u32[]{:S(2)}) copy-start(f32[1,8,128,128]{2,3,1,0:T(8,128)} %get-tuple-element.48) | copy-start | bytes 1572868
  349.1 24.8 %all-to-all-start.6 = ((bf16[8,32,128]{2,1,0:T(8,128)(2,1)}), bf16[8,32,128]{2,1,0:T(8,128)(2,1)}, u32[]{:S(2)}, u32[]{:S(2)}) async-start(bf16[8,32,128]{2,1,0:T(8,128)(2,1)} %bitcast.94), calls=%async_computation.6 | async-start | bytes 131072 | tf_op jit(solution)/shard_map/all_to_all | solution.py:138
  361.2 2.7 copy-start.13
  373.9 19.7 %all-to-all-start.5 = ((bf16[8,32,128]{2,1,0:T(8,128)(2,1)}), bf16[8,32,128]{2,1,0:T(8,128)(2,1)S(1)}, u32[]{:S(2)}, u32[]{:S(2)}) async-start(bf16[8,32,128]{2,1,0:T(8,128)(2,1)} %bitcast.84), calls=%async_computation.5 | async-start | bytes 131072 | tf_op jit(solution)/shard_map/all_to_all | solution.py:137
  393.6 22.1 %all-to-all-start.4 = ((bf16[8,32,1024]{2,1,0:T(8,128)(2,1)}), bf16[8,32,1024]{2,1,0:T(8,128)(2,1)S(1)}, u32[]{:S(2)}, u32[]{:S(2)}) async-start(bf16[8,32,1024]{2,1,0:T(8,128)(2,1)} %bitcast.80), calls=%async_computation.4 | async-start | bytes 1048576 | tf_op jit(solution)/shard_map/all_to_all | solution.py:136
  (18 other events, 29.2 us)
Sparse Core Ops, SparseCore 0:
  66.6 138.4 all-gather.2
  207.3 113.4 all-gather.4
  345.0 449.5 reduce-scatter.3
where the time goes:
time: 805 us; the launch traced here: 803 us
  waiting for transfers between devices  667 us (83%)
  starting transfers between devices  52.9 us (7%)
  local copies, waits for them, and re-layouts  32.1 us (4%)
  matrix products  22.4 us (3%)
  between operations  15.7 us (2%)
  other arithmetic  13.2 us (2%)
    unnamed x4, waiting for transfers between devices  380 us
    all_gather x1, waiting for transfers between devices, body(): lax.all_gather(prefix_values, 'resp', axis=0, tiled=True)  106 us
    all_gather x1, waiting for transfers between devices, body(): lax.all_gather(prefix_keys, 'resp', axis=0, tiled=True)  74.6 us
    all_to_all x1, waiting for transfers between devices, body(): lax.all_to_all(queries, 'tp', split_axis=1, concat_axis=0, tiled=True)  25.4 us
    all_to_all x1, waiting for transfers between devices, body(): lax.all_to_all(out_grad, 'tp', split_axis=1, concat_axis=0, tiled=True)  22.6 us
    all_to_all x1, starting transfers between devices, body(): lax.all_to_all(keys, 'tp', split_axis=1, concat_axis=0, tiled=True)  18.2 us
  transfers between devices with their start and end apart: 10, of which 10 were waited for; matrix products, arithmetic and copies ran while one was open for 5% of the time, Pallas kernels for 0%

commit v1 on v0

v1 whole, which is shorter than its diff:
```python
import functools
import math

import jax
import jax.numpy as jnp
from jax import lax
from jax.experimental import pallas as pl
from jax.experimental.pallas import tpu as pltpu
from jax.sharding import PartitionSpec as P

HD = 128
RCAP = 128
PLEN = 512
PROMPTS = 8
X, Y, ZL, C, ZH = 4, 4, 8, 2, 2
Z = ZL * ZH
REP = 8
QW = REP * HD
LATE = 6
TOK = 32
MESH = pl.DeviceIdType.MESH
F32 = jnp.float32
BF16 = jnp.bfloat16
SCALE = 1.0 / math.sqrt(HD)
SCALE2 = SCALE * math.log2(math.e)


def where_is(x, y, z, c):
    return {"resp": x * (ZL * C) + lax.rem(z, ZL) * C + c, "tp": y * ZH + z // ZL}


def remote(src, dst, send, recv, device):
    return pltpu.make_async_remote_copy(
        src_ref=src, dst_ref=dst, send_sem=send, recv_sem=recv, device_id=device, device_id_type=MESH
    )


def dot_nt(a, b):
    return lax.dot_general(a, b, (((1,), (1,)), ((), ())), preferred_element_type=F32)


def dot_nn(a, b):
    return lax.dot_general(a, b, (((1,), (0,)), ((), ())), preferred_element_type=F32)


def dot_tn(a, b):
    return lax.dot_general(a, b, (((0,), (0,)), ((), ())), preferred_element_type=F32)


ROWS = REP * TOK
CHUNK = 128
CHUNKS = (PLEN + RCAP) // CHUNK


def kernel(
    q_in, k_in, v_in, g_in, pk_in, pv_in, len_in, prompt_in,
    dq_out, dkvr, zr,
    len_s, prompt_s, aux_l, aux_v, aux_s, qs, gs, ks, vs, side, kvrel, rows, kvx, pkb, pvb,
    term, dense, dqs, dkvs, dkrel,
    ra, rb, ra1, rb1, ra2, rb2, xsum, zrel, qh, gh, kk, vv, s_scr, dp_scr, p_scr, b_scr, ds_scr,
    aux_sem, in_sem, r_ss, r_rs, kr_ss, kr_rs, kx_ss, kx_rs,
    near_in, far_in, p_ss, p_rs, z_ss, z_rs, x_ss, x_rs, x2_ss, x2_rs,
    dq_ss, dq_rs, dkv_ss, dkv_rs, dr_ss, dr_rs, df_ss, df_rs,
    rx_ss, rx_rs, rx2_ss, rx2_rs, rz_ss, rz_rs, rl_rs,
):
    r = lax.axis_index("resp")
    t = lax.axis_index("tp")
    x, zl, c = r // (ZL * C), lax.rem(r // C, ZL), lax.rem(r, C)
    y, zh = t // ZH, lax.rem(t, ZH)
    z = zh * ZL + zl
    head = y * C + c
    xr, xl = lax.rem(x + 1, X), lax.rem(x + X - 1, X)
    xo = lax.rem(x + 2, X)
    zr_, zl_ = lax.rem(z + 1, Z), lax.rem(z + Z - 1, Z)
    here = where_is(x, y, z, c)

    z4 = (lax.rem(z + 4, Z), lax.rem(z + Z - 4, Z))
    y_odd = lax.rem(y, 2) == 1

    loads = [
        pltpu.make_async_copy(k_in, ks, in_sem.at[0]),
        pltpu.make_async_copy(v_in, vs, in_sem.at[1]),
        pltpu.make_async_copy(q_in, qs, in_sem.at[2]),
        pltpu.make_async_copy(g_in, gs, in_sem.at[3]),
    ]
    for cp in loads:
        cp.start()
    ints = [
        pltpu.make_async_copy(len_in, len_s, aux_sem.at[0]),
        pltpu.make_async_copy(prompt_in, prompt_s, aux_sem.at[3]),
    ]
    for cp in ints:
        cp.start()

    barrier = pltpu.get_barrier_semaphore()

    def greet(x_, y_, z_, c_):
        pl.semaphore_signal(barrier, inc=1, device_id=where_is(x_, y_, z_, c_), device_id_type=MESH)

    def greet_y(i, carry):
        y_ = lax.rem(y + i, Y)
        greet(x, y_, z, c)
        greet(x, y_, z, 1 - c)
        return carry

    lax.fori_loop(1, Y, greet_y, 0)
    greet(xr, y, z, c)
    greet(xl, y, z, c)
    greet(xo, y, z, c)
    greet(x, y, z, 1 - c)
    z2 = (lax.rem(z + 2, Z), lax.rem(z + Z - 2, Z))
    for z_ in (zr_, zl_) + z2:
        greet(x, y, z_, c)
        greet(x, y, z_, 1 - c)

    def tell(sem):
        for i in (0, 1):
            pl.semaphore_signal(sem.at[i], inc=1, device_id=where_is(x, y, z2[i], c), device_id_type=MESH)

    def told(sem):
        for i in (0, 1):
            pl.semaphore_wait(sem.at[i], 1)

    for cp in loads:
        cp.wait()
    for h in range(8):
        side[h, :, :QW] = qs[:, h * QW : (h + 1) * QW]
        side[h, :, QW : 2 * QW] = gs[:, h * QW : (h + 1) * QW]
        side[h, :, 2 * QW : 2 * QW + HD] = ks[:, h * HD : (h + 1) * HD]
        side[h, :, 2 * QW + HD :] = vs[:, h * HD : (h + 1) * HD]

    pl.semaphore_wait(barrier, 2 * (Y - 1) + 3 + 1 + 8)
    tell(near_in)

    def chunk(w, x_, zl_src):
        return prefix[w].at[x_ * 2 + zl_src // 4, lax.rem(zl_src, 4)]

    own_core = c == zh
    prefix_in = (pk_in, pv_in)
    prefix = (pkb, pvb)

    def mine_near(w):
        return pltpu.make_async_copy(prefix_in[w], chunk(w, x, zl).at[c], p_ss.at[w, 0])

    def mine_far(w, i):
        z_ = (z, zr_, z2[0], zl_, z2[1])[i]
        ref = chunk(w, x, zl).at[c]
        return remote(prefix_in[w], ref, p_ss.at[w, i], p_rs.at[w, zl, c], where_is(x, y, z_, zh))

    def mine_send(w):
        for i in (2, 4, 1, 3):
            mine_far(w, i).start()

        @pl.when(own_core)
        def _():
            mine_near(w).start()

        @pl.when(jnp.logical_not(own_core))
        def _():
            mine_far(w, 0).start()

    def halves_wait(w, s):
        for half in (0, 1):
            ref = chunk(w, x, s).at[half]
            remote(prefix_in[w], ref, p_ss.at[w, 0], p_rs.at[w, s, half], here).wait_recv()

    def mine_wait(w):
        @pl.when(own_core)
        def _():
            mine_near(w).wait()
            remote(prefix_in[w], chunk(w, x, zl).at[1 - c], p_ss.at[w, 0], p_rs.at[w, zl, 1 - c], here).wait_recv()

    mine_send(0)
    mine_send(1)

    def slot_of(y_, c_):
        return ((y_ // 2) * 2 + c_) * 2 + lax.rem(y_, 2)

    my_slot = slot_of(y, c)

    def row_copy(dy, dc):
        y_, c_ = lax.rem(y + dy, Y), lax.rem(c + dc, C)
        return remote(
            side.at[y_ * C + c_], rows.at[my_slot], r_ss.at[dy * 2 + dc], r_rs.at[my_slot], where_is(x, y_, z, c_)
        )

    def unseen(zh_src, odd):
        return jnp.logical_and(zh_src == 1, odd)

    def rel_copy(kv, way):
        src = side.at[pl.ds(4 * way, 4), :, pl.ds(2 * QW + kv * HD, HD)]
        return remote(src, kvrel.at[kv, way], kr_ss.at[kv, way], kr_rs.at[kv, way], where_is(x, y, z4[way], c))

    def rel_src(way):
        return z4[1 - way] // ZL

    def rel_on(kv, way):
        return [
            remote(
                kvrel.at[kv, way, i],
                kvx.at[kv, my_slot],
                kx_ss.at[kv, way * 4 + i],
                kx_rs.at[kv, my_slot],
                where_is(x, 2 * way + i // 2, z4[way], i % 2),
            )
            for i in range(4)
        ]

    def rel_start(kv):
        @pl.when(jnp.logical_not(unseen(zh, y_odd)))
        def _():
            for way in (0, 1):
                rel_copy(kv, way).start()

    def rel_pass(kv):
        for way in (0, 1):

            @pl.when(jnp.logical_not(unseen(rel_src(way), y_odd)))
            def _():
                rel_copy(kv, way).wait_recv()
                for cp in rel_on(kv, way):
                    cp.start()

    def kvx_wait(kv):
        for y_ in range(Y):
            for c_ in range(C):

                @pl.when(jnp.logical_not(unseen(1 - zh, y_ % 2 == 1)))
                def _():
                    ref = kvx.at[kv, slot_of(y_, c_)]
                    remote(ref, ref, kx_ss.at[kv, 0], kx_rs.at[kv, slot_of(y_, c_)], here).wait_recv()

    far = [(dy, dc) for dc in (0, 1) for dy in (1, 3, 2, 0) if (dy, dc) != (0, 0)]

    def y_start(*pairs):
        for dy, dc in pairs:
            row_copy(dy, dc).start()

    y_start((1, 0), (3, 0))

    @pl.when(jnp.logical_not(own_core))
    def _():
        y_start((2, 0), (1, 1), (3, 1), (2, 1), (0, 1))

    own = pltpu.make_async_copy(side.at[head], rows.at[my_slot], r_ss.at[0])
    own.start()

    for cp in ints:
        cp.wait()
    lane = lax.broadcasted_iota(jnp.int32, (8, 128), 1)
    aux_l[...] = jnp.where(
        lane == 0,
        prompt_s[0],
        jnp.where(lane == 1, prompt_s[1], jnp.where(lane == 2, len_s[0], len_s[1])),
    )
    aux_own = pltpu.make_async_copy(aux_l, aux_v.at[c], aux_sem.at[0])
    aux_own.start()
    aux_far = remote(aux_l, aux_v.at[c], aux_sem.at[1], aux_sem.at[2], where_is(x, y, z, 1 - c))
    aux_far.start()

    def z_copy(w, way, far_, s):
        up_dev = where_is(x, y, lax.rem(z + 1 + far_, Z), c)
        down_dev = where_is(x, y, lax.rem(z + Z - 1 - far_, Z), c)
        ref = chunk(w, x, s)
        return remote(ref, ref, z_ss.at[w, way, far_, s], z_rs.at[w, s], up_dev if way == 0 else down_dev)

    def x_copy(w, way, s):
        ref, dev = chunk(w, x, s), where_is(xr if way == 0 else xl, y, z, c)
        return remote(ref, ref, x_ss.at[w, way, s], x_rs.at[w, way, s], dev)

    def x_arrived(w, way, s):
        ref = chunk(w, xl if way == 0 else xr, s)
        return remote(ref, ref, x_ss.at[w, way, s], x_rs.at[w, way, s], here)

    def x2_copy(w, way, s):
        ref, dev = chunk(w, xl if way == 0 else xr, s).at[way], where_is(xr if way == 0 else xl, y, z, c)
        return remote(ref, ref, x2_ss.at[w, way, s], x2_rs.at[w, way, s], dev)

    def x3_copy(w, s):
        ref = chunk(w, x, s)
        return remote(ref, ref, x2_ss.at[w, 0, s], x2_rs.at[w, 0, s], where_is(xo, y, z, c))

    def x3_arrived(w, s):
        ref = chunk(w, xo, s)
        return remote(ref, ref, x2_ss.at[w, 0, s], x2_rs.at[w, 0, s], here)

    def x2_arrived(w, way, s):
        ref = chunk(w, xo, s).at[way]
        return remote(ref, ref, x2_ss.at[w, way, s], x2_rs.at[w, way, s], here)

    def source(way, k):
        s = lax.rem(z + (Z - k if way == 0 else k), Z)
        return s // ZL == c, lax.rem(s, ZL)

    def x_start(w, s):
        x_copy(w, 0, s).start()
        x_copy(w, 1, s).start()

    def forwards(w, way, j, s):
        return [z_copy(w, way, i, s) for i in (2, 1, 0) if not (j == 2 and way == 1 and i == 2)]

    def stop(w, j):
        for way in (0, 1):
            live, s = source(way, 3 * j - 1 if j else 0)

            @pl.when(live)
            def _():
                if j == 1:
                    halves_wait(w, s)
                elif j == 2:
                    z_copy(w, way, 0, s).wait_recv()
                if j > 0:
                    for cp in forwards(w, way, j, s):
                        cp.start()

        for way in (0, 1):
            live, s = source(way, 3 * j - 1 if j else 0)

            @pl.when(live)
            def _():
                if j > 0 or way == 0:
                    x_start(w, s)

        for k in ((), (1,), (3, 4))[j]:
            for way in (0, 1):
                arrive(w, way, k)

    def arrive(w, way, k):
        live, s = source(way, k)

        @pl.when(live)
        def _():
            if k == 1:
                halves_wait(w, s)
            else:
                z_copy(w, way, 0, s).wait_recv()
            x_start(w, s)
            if k >= LATE:
                x3_copy(w, s).start()

    def stop_sent(w, j):
        for way in (0, 1):
            live, s = source(way, 3 * j - 1)

            @pl.when(live)
            def _():
                for cp in forwards(w, way, j, s):
                    cp.wait_send()

    def last_arrivals(w):
        for way, k in ((0, 6), (1, 6), (0, 7), (1, 7), (0, 8)):
            arrive(w, way, k)

    def pass_on(w, way, k):
        live, s = source(way, k)

        @pl.when(live)
        def _():
            for x_way in (0, 1):
                x_arrived(w, x_way, s).wait_recv()
                x2_copy(w, x_way, s).start()

    def all_on(w, low, high):
        for k in range(low, high):
            pass_on(w, 0, k)
            if 0 < k < 8:
                pass_on(w, 1, k)

    all_sources = [(way, k) for k in range(9) for way in (0, 1) if way == 0 or 0 < k < 8]

    def x2_wait(w):
        for way, k in all_sources:
            live, s = source(way, k)

            @pl.when(live)
            def _():
                if k >= LATE:
                    x_arrived(w, 0, s).wait_recv()
                    x_arrived(w, 1, s).wait_recv()
                    x3_arrived(w, s).wait_recv()
                else:
                    x2_arrived(w, 0, s).wait_recv()
                    x2_arrived(w, 1, s).wait_recv()

    def y_between(*pairs):
        @pl.when(own_core)
        def _():
            y_start(*pairs)

    mine_wait(0)
    stop(0, 0)
    y_between((2, 0), (1, 1), (3, 1))
    mine_wait(1)
    told(near_in)
    tell(far_in)
    stop(0, 1)
    stop(1, 0)
    told(far_in)
    rel_start(0)
    y_between((2, 1), (0, 1))
    stop(0, 2)
    stop(1, 1)
    rel_pass(0)
    rel_start(1)
    last_arrivals(0)
    stop(1, 2)
    rel_pass(1)
    all_on(0, 0, LATE)
    last_arrivals(1)

    for dy, dc in far:
        ref = rows.at[slot_of(lax.rem(y + dy, Y), lax.rem(c + dc, C))]
        remote(ref, ref, r_ss.at[0], r_rs.at[slot_of(lax.rem(y + dy, Y), lax.rem(c + dc, C))], here).wait_recv()
    kvx_wait(0)
    own.wait()
    aux_own.wait()
    remote(aux_l, aux_v.at[1 - c], aux_sem.at[1], aux_sem.at[2], here).wait_recv()

    to_smem = pltpu.make_async_copy(aux_v, aux_s, aux_sem.at[3])
    to_smem.start()
    to_smem.wait()

    x2_wait(0)

    def q_cols(ref, h):
        return ref.at[:, pl.ds(pl.multiple_of(h * QW, QW), QW)]

    def dq_copy(sl):
        rho = sl // 2
        y_, c_ = (rho // 2) * 2 + lax.rem(sl, 2), lax.rem(rho, 2)
        dst = q_cols(dq_out, head)
        return (
            sl == my_slot,
            remote(dqs.at[sl], dst, dq_ss.at[sl], dq_rs.at[head], where_is(x, y_, z, c_)),
            pltpu.make_async_copy(dqs.at[sl], dst, dq_ss.at[sl]),
        )

    def dkv_copy(rho, yb):
        y_, c_ = (rho // 2) * 2 + yb, lax.rem(rho, 2)
        i = dk_slot(rho, yb)
        src, dst = dkvs.at[zh, i], dkvr.at[zh, head]
        return (
            jnp.logical_and(y_ == y, c_ == c),
            remote(src, dst, dkv_ss.at[i], dkv_rs.at[zh * 8 + head], where_is(x, y_, z, c_)),
            pltpu.make_async_copy(src, dst, dkv_ss.at[i]),
        )

    def dk_slot(rho, yb):
        return (rho // 2) * 4 + yb * 2 + lax.rem(rho, 2)

    def drel_copy(kv, way, yb):
        dev = where_is(x, y, jnp.where(way == 0, z4[0], z4[1]), c)
        src = dkvs.at[1 - zh, pl.ds(way * 4 + yb * 2, 2), kv]
        return remote(src, dkrel.at[kv, way, yb], dr_ss.at[kv, way, yb], dr_rs.at[kv, way, yb], dev)

    def drel_start(kv, way):
        drel_copy(kv, way, 0).start()

        @pl.when(zh == 1)
        def _():
            drel_copy(kv, way, 1).start()

    def drel_on(kv, way, yb):
        zs = rel_src(way)
        return [
            remote(
                dkrel.at[kv, way, yb, i],
                dkvr.at[zs, head, kv],
                df_ss.at[kv, way, yb * 2 + i],
                df_rs.at[kv, head],
                where_is(x, 2 * way + yb, z4[way], i),
            )
            for i in (0, 1)
        ]

    def drel_pass(kv, way):
        drel_copy(kv, way, 0).wait_recv()
        for cp in drel_on(kv, way, 0):
            cp.start()

        @pl.when(rel_src(way) == 1)
        def _():
            drel_copy(kv, way, 1).wait_recv()
            for cp in drel_on(kv, way, 1):
                cp.start()

    def send(copies):
        local, far_cp, near_cp = copies

        @pl.when(local)
        def _():
            near_cp.start()

        @pl.when(jnp.logical_not(local))
        def _():
            far_cp.start()

    def sent(copies):
        local, far_cp, near_cp = copies

        @pl.when(local)
        def _():
            near_cp.wait()

        @pl.when(jnp.logical_not(local))
        def _():
            far_cp.wait_send()

    def fold(a, op):
        return op(a.reshape(CHUNK // 8, 8, ROWS), 0)

    def keys_of(kv, prompt, rho, to):
        to[:PLEN] = prefix[kv][prompt].reshape(PLEN, HD)
        for b in (0, 1):
            i = rho * 2 + b
            near = pl.ds(pl.multiple_of(PLEN + (2 * b + zh) * TOK, TOK), TOK)
            over = pl.ds(pl.multiple_of(PLEN + (2 * b + 1 - zh) * TOK, TOK), TOK)
            low = 2 * QW + kv * HD
            to[near] = rows[i, :, low : low + HD]
            crossed = kvx[kv, i].astype(F32)
            if b == 1:
                crossed = jnp.where(zh == 1, crossed, 0.0)
            to[over] = crossed.astype(BF16)

    def leave(kv, rho, grad):
        for i in range(4):
            for ct in (0, 1):
                low = (i * 2 + ct) * 64
                term[kv, rho, ct, i] = grad[low : low + 64].astype(BF16)
        for tb in range(4):
            low = PLEN + tb * TOK
            dkvs[tb % 2, dk_slot(rho, tb // 2), kv] = grad[low : low + TOK].astype(BF16)

    def weigh(rho, carry):
        prompt = aux_s[lax.rem(rho, 2), 0, rho // 2]
        length = aux_s[lax.rem(rho, 2), 0, 2 + rho // 2]
        k_rho = kk.at[rho]
        keys_of(0, prompt, rho, k_rho)
        acc = []
        for b in (0, 1):
            i = rho * 2 + b
            qa, ga = rows[i, :, :QW], rows[i, :, QW : 2 * QW]
            tok = lax.broadcasted_iota(jnp.int32, (TOK, HD), 0) + (64 * b + TOK * zh)
            keep = jnp.where(tok < length, 1.0, 0.0)
            q = jnp.concatenate([qa[:, h * HD : (h + 1) * HD] for h in range(REP)], axis=0)
            g = jnp.concatenate(
                [(ga[:, h * HD : (h + 1) * HD].astype(F32) * keep).astype(BF16) for h in range(REP)], axis=0
            )
            qh[i] = q
            gh[i] = g
            top = jnp.full((8, ROWS), -jnp.inf, F32)
            for n in range(CHUNKS):
                at = slice(n * CHUNK, (n + 1) * CHUNK)
                s = dot_nt(k_rho[at], q)
                if n == CHUNKS - 1:
                    col = lax.broadcasted_iota(jnp.int32, (CHUNK, ROWS), 1)
                    key = lax.broadcasted_iota(jnp.int32, (CHUNK, ROWS), 0)
                    s = jnp.where(key <= lax.rem(col, TOK) + (64 * b + TOK * zh), s, -jnp.inf)
                s_scr[b, at] = s
                top = jnp.maximum(top, fold(s, jnp.max))
            top = jnp.max(top, 0, keepdims=True)
            total = jnp.zeros((8, ROWS), F32)
            for n in range(CHUNKS):
                at = slice(n * CHUNK, (n + 1) * CHUNK)
                e = jnp.exp2((s_scr[b, at] - top) * SCALE2)
                s_scr[b, at] = e
                total = total + fold(e, jnp.sum)
            inv = 1.0 / jnp.sum(total, 0, keepdims=True)
            for n in range(CHUNKS):
                at = slice(n * CHUNK, (n + 1) * CHUNK)
                p = s_scr[b, at] * inv
                p_scr[i, at] = p
                b_scr[b, at] = p.astype(BF16)
            acc.append(dot_nn(b_scr[b], g))
        leave(1, rho, acc[0] + acc[1])

        @pl.when(lax.rem(rho, 2) == 1)
        def _():
            drel_start(1, rho // 2)

        @pl.when(rho == 0)
        def _():
            all_on(1, 0, 3)

        @pl.when(rho == 1)
        def _():
            all_on(1, 3, LATE)

        return carry

    def differentiate(rho, carry):
        prompt = aux_s[lax.rem(rho, 2), 0, rho // 2]
        keys_of(1, prompt, rho, vv)
        acc = []
        for b in (0, 1):
            i = rho * 2 + b
            mixed = jnp.zeros((8, ROWS), F32)
            for n in range(CHUNKS):
                at = slice(n * CHUNK, (n + 1) * CHUNK)
                dp = dot_nt(vv[at], gh[i])
                dp_scr[b, at] = dp
                mixed = mixed + fold(p_scr[i, at] * dp, jnp.sum)
            delta = jnp.sum(mixed, 0, keepdims=True)
            for n in range(CHUNKS):
                at = slice(n * CHUNK, (n + 1) * CHUNK)
                ds_scr[i, at] = (p_scr[i, at] * (dp_scr[b, at] - delta)).astype(BF16)
            acc.append(dot_nn(ds_scr[i], qh[i]))
        leave(0, rho, (acc[0] + acc[1]) * SCALE)

        @pl.when(lax.rem(rho, 2) == 1)
        def _():
            drel_start(0, rho // 2)

        for b in (0, 1):
            send(dkv_copy(rho, b))

        @pl.when(rho == 2)
        def _():
            for way in (0, 1):
                drel_pass(1, way)

        first(1, order(rho))

        @pl.when(rho >= 2)
        def _():
            second(1, order(rho - 2))

        return carry

    def query_grads(rho, carry):
        for b in (0, 1):
            i = rho * 2 + b
            dq = (dot_tn(kk[rho], ds_scr[i]) * SCALE).T.astype(BF16)
            for h in range(REP):
                dqs[i, :, h * HD : (h + 1) * HD] = dq[h * TOK : (h + 1) * TOK]
            send(dq_copy(i))
        return carry

    def part(w, x_, n, half):
        return dense.at[w, x_ * 2 + n // 2, half, pl.ds(lax.rem(n, 2) * 2, 2)]

    def own_part(w, x_, n, half):
        return dense[w, x_ * 2 + n // 2, half, pl.ds(lax.rem(n, 2) * 2, 2)].astype(F32)

    def rx_copy(w, way, n):
        if way == 0:
            src, dst, dev = part(w, xo, n, 0), ra.at[w, n], where_is(xr, y, z, c)
        elif way == 1:
            src, dst, dev = part(w, xo, n, 1), rb.at[w, n], where_is(xl, y, z, c)
        elif way == 2:
            src, dst, dev = part(w, xr, n, 1), rb1.at[w, n], where_is(xr, y, z, c)
        else:
            src, dst, dev = part(w, xl, n, 0), ra1.at[w, n], where_is(xl, y, z, c)
        return remote(src, dst, rx_ss.at[w, way, n], rx_rs.at[w, way, n], dev)

    def rx2_copy(w, way, n):
        if way == 0:
            src, dst, dev = ra.at[w, n], ra2.at[w, n], where_is(xr, y, z, c)
        else:
            src, dst, dev = rb.at[w, n], rb2.at[w, n], where_is(xl, y, z, c)
        return remote(src, dst, rx2_ss.at[w, way, n], rx2_rs.at[w, way, n], dev)

    rising = (zh != c) == (zl < 4)

    def order(i):
        n = lax.rem(i, 2) * 2 + i // 2
        return jnp.where(rising, n, 3 - n)

    def spread_all(w):
        def spread_half(i, carry):
            ip = jnp.where(rising, i, 1 - i)
            two = pl.ds(ip * 2, 2)

            def spread(p, carry):
                acc = jnp.zeros((2, 2, 64, HD), F32)
                for rho in range(4):
                    hit = aux_s[rho % 2, 0, rho // 2] == p
                    acc = acc + jnp.where(hit, term[w, rho, :, two].astype(F32), 0.0)
                dense[w, p, :, two] = acc.astype(BF16)
                return carry

            lax.fori_loop(0, PROMPTS, spread, 0)
            for j in (0, 1):
                for way in (0, 1):
                    rx_copy(w, way, order(2 * i + j)).start()
            return carry

        lax.fori_loop(0, 2, spread_half, 0)

    def z_dist(zt):
        return lax.rem(c * ZL + zt - z + 23, Z) - 7

    def z_direct(w, zt, ct, d):
        src, dst, zd = xsum.at[w, zt, ct], zr.at[w, d + 4], c * ZL + zt
        return (
            jnp.logical_and(d == 0, ct == c),
            remote(src, dst, rz_ss.at[w, ct, zt], rz_rs.at[w, d + 4], where_is(x, y, zd, ct)),
            pltpu.make_async_copy(src, dst, rz_ss.at[w, ct, zt]),
        )

    def z_stop(w, zt, d):
        up_ = d > 0
        zd = lax.rem(z + Z + jnp.where(up_, d - 4, d + 4), Z)
        i = jnp.where(up_, d, -d) - 5
        return remote(xsum.at[w, zt], zrel.at[w, i], rz_ss.at[w, 0, zt], rl_rs.at[w, i], where_is(x, y, zd, c))

    def is_far(d):
        return jnp.logical_or(d > 4, d < -4)

    def is_near(d):
        return jnp.logical_and(d < 4, d > -4)

    def first(w, n):
        rx_copy(w, 0, n).wait_recv()
        ra[w, n] = (ra[w, n].astype(F32) + own_part(w, xr, n, 0)).astype(BF16)
        rx2_copy(w, 0, n).start()
        rx_copy(w, 2, n).start()
        rx_copy(w, 1, n).wait_recv()
        rb[w, n] = (rb[w, n].astype(F32) + own_part(w, xl, n, 1)).astype(BF16)
        rx2_copy(w, 1, n).start()
        rx_copy(w, 3, n).start()

    def second(w, n):
        rx_copy(w, 3, n).wait_recv()
        rx2_copy(w, 0, n).wait_recv()
        one = own_part(w, x, n, 0) + ra1[w, n].astype(F32) + ra2[w, n].astype(F32)
        rx_copy(w, 2, n).wait_recv()
        rx2_copy(w, 1, n).wait_recv()
        two = own_part(w, x, n, 1) + rb1[w, n].astype(F32) + rb2[w, n].astype(F32)
        for i in (0, 1):
            zt = 2 * n + i
            xsum[w, zt, 0] = one[i].astype(BF16)
            xsum[w, zt, 1] = two[i].astype(BF16)
            d = z_dist(zt)

            @pl.when(is_near(d))
            def _():
                for ct in (0, 1):
                    send(z_direct(w, zt, ct, d))

            @pl.when(is_far(d))
            def _():
                z_stop(w, zt, d).start()

    zt_stop = lax.rem(zl + 4, ZL)
    d_stop = z_dist(zt_stop)

    def stop_sum(w):
        def stop_wait(i, carry):
            @pl.when(jnp.logical_or(i < 3, d_stop > 0))
            def _():
                remote(zrel.at[w, i], zrel.at[w, i], rz_ss.at[w, 0, 0], rl_rs.at[w, i], here).wait_recv()

            return carry

        lax.fori_loop(0, 4, stop_wait, 0)
        for ct in (0, 1):
            three = xsum[w, zt_stop, ct].astype(F32)
            for i in range(3):
                three = three + zrel[w, i, ct].astype(F32)

            @pl.when(d_stop > 0)
            def _():
                xsum[w, zt_stop, ct] = (three + zrel[w, 3, ct].astype(F32)).astype(BF16)

            @pl.when(d_stop < 0)
            def _():
                xsum[w, zt_stop, ct] = three.astype(BF16)

            z_direct(w, zt_stop, ct, d_stop)[1].start()

    lax.fori_loop(0, 4, weigh, 0)
    spread_all(1)
    x2_wait(1)
    kvx_wait(1)
    lax.fori_loop(0, 4, differentiate, 0)
    spread_all(0)
    drel_pass(0, 0)
    lax.fori_loop(0, 4, query_grads, 0)
    second(1, order(2))
    second(1, order(3))

    def last(i, carry):
        @pl.when(i < 4)
        def _():
            first(0, order(i))

        @pl.when(i == 1)
        def _():
            drel_pass(0, 1)

        @pl.when(i == 2)
        def _():
            stop_sum(1)

        @pl.when(i >= 1)
        def _():
            second(0, order(i - 1))

        return carry

    lax.fori_loop(0, 5, last, 0)
    stop_sum(0)

    def dkv_wait(h, carry):
        near = dkvr.at[zh, h]

        @pl.when(h != head)
        def _():
            remote(near, near, dkv_ss.at[0], dkv_rs.at[zh * 8 + h], here).wait_recv()

        @pl.when(jnp.logical_not(unseen(zh, y_odd)))
        def _():
            for kv in (0, 1):
                over = dkvr.at[1 - zh, h, kv]
                remote(over, over, dkv_ss.at[0], df_rs.at[kv, h], here).wait_recv()

        return carry

    def dkv_sent(i, carry):
        for yb in (0, 1):
            sent(dkv_copy(i, yb))
        return carry

    lax.fori_loop(0, 4, dkv_sent, 0)
    lax.fori_loop(0, 8, dkv_wait, 0)
    def z_sent(i, carry):
        w, n = i // ZL, lax.rem(i, ZL)
        d = z_dist(n)

        @pl.when(is_far(d))
        def _():
            z_stop(w, n, d).wait_send()

        @pl.when(jnp.logical_not(is_far(d)))
        def _():
            for ct in (0, 1):
                sent(z_direct(w, n, ct, d))

        return carry

    def z_wait(i, carry):
        for w in (0, 1):

            @pl.when(jnp.logical_not(jnp.logical_and(own_core, i == 4)))
            def _():
                remote(zr.at[w, i], zr.at[w, i], rz_ss.at[w, 0, 0], rz_rs.at[w, i], here).wait_recv()

        return carry

    lax.fori_loop(0, 2 * ZL, z_sent, 0)
    lax.fori_loop(0, 9, z_wait, 0)

    def dq_wait(h, carry):
        @pl.when(h != head)
        def _():
            ref = q_cols(dq_out, h)
            remote(ref, ref, dq_ss.at[0], dq_rs.at[h], here).wait_recv()

        return carry

    def dq_sent(i, carry):
        sent(dq_copy(i))
        return carry

    lax.fori_loop(0, 8, dq_sent, 0)
    lax.fori_loop(0, 8, dq_wait, 0)
    aux_far.wait_send()
    for dy, dc in far:
        row_copy(dy, dc).wait_send()

    @pl.when(jnp.logical_not(unseen(zh, y_odd)))
    def _():
        for kv in (0, 1):
            for way in (0, 1):
                rel_copy(kv, way).wait_send()

    for way in (0, 1):

        @pl.when(jnp.logical_not(unseen(rel_src(way), y_odd)))
        def _():
            for cp in rel_on(0, way) + rel_on(1, way):
                cp.wait_send()

        for kv in (0, 1):
            drel_copy(kv, way, 0).wait_send()
            for cp in drel_on(kv, way, 0):
                cp.wait_send()

        @pl.when(zh == 1)
        def _():
            for kv in (0, 1):
                drel_copy(kv, way, 1).wait_send()

        @pl.when(rel_src(way) == 1)
        def _():
            for kv in (0, 1):
                for cp in drel_on(kv, way, 1):
                    cp.wait_send()

    for w in (0, 1):
        for i in (1, 2, 3, 4):
            mine_far(w, i).wait_send()

        @pl.when(jnp.logical_not(own_core))
        def _():
            mine_far(w, 0).wait_send()

    for w in (0, 1):
        for j in (1, 2):
            stop_sent(w, j)

    def x_sent(s, carry):
        for w in (0, 1):
            for way in (0, 1):
                x_copy(w, way, s).wait_send()
        return carry

    lax.fori_loop(0, ZL, x_sent, 0)
    for w in (0, 1):
        for way, k in all_sources:
            live, s = source(way, k)

            @pl.when(live)
            def _():
                if k >= LATE:
                    x3_copy(w, s).wait_send()
                else:
                    x2_copy(w, 0, s).wait_send()
                    x2_copy(w, 1, s).wait_send()

    def rx_sent(n, carry):
        for w in (0, 1):
            for way in range(4):
                rx_copy(w, way, n).wait_send()
            for way in (0, 1):
                rx2_copy(w, way, n).wait_send()
        return carry

    lax.fori_loop(0, 4, rx_sent, 0)


def finish(dq_in, dkvr_in, zr_in, dq_out, dk_out, dv_out, gpk_out, gpv_out, dq, dkvr, zr, sem):
    loads = [
        pltpu.make_async_copy(dq_in, dq, sem.at[0]),
        pltpu.make_async_copy(dkvr_in, dkvr, sem.at[1]),
        pltpu.make_async_copy(zr_in, zr, sem.at[2]),
    ]
    for cp in loads:
        cp.start()
    loads[0].wait()
    store = pltpu.make_async_copy(dq, dq_out, sem.at[3])
    store.start()
    loads[1].wait()
    loads[2].wait()
    t = lax.axis_index("tp")
    near = lax.rem(t, ZH)
    whole = jnp.where(jnp.logical_and(near == 1, lax.rem(t // ZH, 2) == 1), 0, 1)
    for h in range(8):
        over = jnp.where(whole == 1, dkvr[1 - near, h].astype(F32), 0.0)
        summed = dkvr[near, h].astype(F32) + over
        dk_out[:, h * HD : (h + 1) * HD] = summed[0].astype(BF16)
        dv_out[:, h * HD : (h + 1) * HD] = summed[1].astype(BF16)
    for w, ref in ((0, gpk_out), (1, gpv_out)):
        all_z = zr[w, 0].astype(F32)
        for i in range(1, 9):
            all_z = all_z + zr[w, i].astype(F32)
        ref[...] = all_z.astype(BF16)
    store.wait()


def body(queries, keys, values, out_grad, prefix_keys, prefix_values, lengths, prompt_of):
    dma = pltpu.SemaphoreType.DMA
    vm = lambda *shape: pltpu.VMEM(shape, BF16)
    out = lambda *shape: jax.ShapeDtypeStruct(shape, BF16)
    hbm = pl.BlockSpec(memory_space=pl.ANY)
    vmem = pl.BlockSpec(memory_space=pltpu.VMEM)
    wide = 2 * QW + 2 * HD
    dq, dkvr, zr = pl.pallas_call(
        kernel,
        out_shape=(out(TOK, 8 * REP * HD), out(2, 8, 2, TOK, HD), out(2, 9, 64, HD)),
        in_specs=[hbm] * 8,
        out_specs=(hbm,) * 3,
        scratch_shapes=[
            pltpu.SMEM((2,), jnp.int32),
            pltpu.SMEM((2,), jnp.int32),
            pltpu.VMEM((8, 128), jnp.int32),
            pltpu.VMEM((2, 8, 128), jnp.int32),
            pltpu.SMEM((2, 8, 128), jnp.int32),
            vm(TOK, 8 * QW),
            vm(TOK, 8 * QW),
            vm(TOK, 8 * HD),
            vm(TOK, 8 * HD),
            vm(8, TOK, wide),
            vm(2, 2, 4, TOK, HD),
            vm(8, TOK, wide),
            vm(2, 8, TOK, HD),
            vm(8, 4, 2, 64, HD),
            vm(8, 4, 2, 64, HD),
            vm(2, 4, 2, 4, 64, HD),
            vm(2, 8, 2, 4, 64, HD),
            vm(8, TOK, REP * HD),
            vm(2, 8, 2, TOK, HD),
            vm(2, 2, 2, 2, TOK, HD),
            vm(2, 4, 2, 64, HD),
            vm(2, 4, 2, 64, HD),
            vm(2, 4, 2, 64, HD),
            vm(2, 4, 2, 64, HD),
            vm(2, 4, 2, 64, HD),
            vm(2, 4, 2, 64, HD),
            vm(2, 8, 2, 64, HD),
            vm(2, 4, 2, 64, HD),
            vm(8, ROWS, HD),
            vm(8, ROWS, HD),
            vm(4, PLEN + RCAP, HD),
            vm(PLEN + RCAP, HD),
            pltpu.VMEM((2, PLEN + RCAP, ROWS), F32),
            pltpu.VMEM((2, PLEN + RCAP, ROWS), F32),
            pltpu.VMEM((8, PLEN + RCAP, ROWS), F32),
            vm(2, PLEN + RCAP, ROWS),
            vm(8, PLEN + RCAP, ROWS),
            dma((4,)),
            dma((4,)), dma((8,)), dma((8,)), dma((2, 2)), dma((2, 2)), dma((2, 8)), dma((2, 8)),
            pltpu.SemaphoreType.REGULAR((2,)), pltpu.SemaphoreType.REGULAR((2,)),
            dma((2, 5)), dma((2, 8, 2)),
            dma((2, 2, 3, 8)), dma((2, 8)), dma((2, 2, 8)), dma((2, 2, 8)), dma((2, 2, 8)), dma((2, 2, 8)),
            dma((8,)), dma((8,)), dma((8,)), dma((16,)), dma((2, 2, 2)), dma((2, 2, 2)), dma((2, 2, 4)), dma((2, 8)),
            dma((2, 4, 4)), dma((2, 4, 4)), dma((2, 2, 4)), dma((2, 2, 4)),
            dma((2, 2, 8)), dma((2, 9)), dma((2, 4)),
        ],
        compiler_params=pltpu.CompilerParams(
            collective_id=0, has_side_effects=True, vmem_limit_bytes=62 * 1024 * 1024
        ),
        cost_estimate=pl.CostEstimate(flops=2_000_000_000, bytes_accessed=4_000_000, transcendentals=1_400_000),
    )(queries, keys, values, out_grad, prefix_keys, prefix_values, lengths, prompt_of)
    return pl.pallas_call(
        finish,
        out_shape=(
            jax.ShapeDtypeStruct(queries.shape, BF16),
            jax.ShapeDtypeStruct(keys.shape, BF16),
            jax.ShapeDtypeStruct(values.shape, BF16),
            jax.ShapeDtypeStruct(prefix_keys.shape, BF16),
            jax.ShapeDtypeStruct(prefix_values.shape, BF16),
        ),
        in_specs=[hbm] * 3,
        out_specs=(hbm,) + (vmem,) * 4,
        scratch_shapes=[vm(TOK, 8 * REP * HD), vm(2, 8, 2, TOK, HD), vm(2, 9, 64, HD), dma((4,))],
        compiler_params=pltpu.CompilerParams(vmem_limit_bytes=62 * 1024 * 1024),
        name="finish",
    )(dq, dkvr, zr)


def solution(mesh):
    in_specs = (
        P(("resp", "tp"), None),
        P(("resp", "tp"), None),
        P(("resp", "tp"), None),
        P(("resp", "tp"), None),
        P("resp", "tp"),
        P("resp", "tp"),
        P("resp"),
        P("resp"),
    )
    out_specs = (
        P(("resp", "tp"), None),
        P(("resp", "tp"), None),
        P(("resp", "tp"), None),
        P("resp", "tp"),
        P("resp", "tp"),
    )
    return jax.shard_map(body, mesh=mesh, in_specs=in_specs, out_specs=out_specs, check_vma=False)
```

time: 805 us -> 86.1 us (0.11)
  the two profiles are of different devices: /device:TPU:8 before, /device:TPU:49 now
where the time goes in v1:
time: 86.1 us; the launch traced here: 85.9 us
  Pallas kernels  85.2 us (99%)
    pallas_call x1, Pallas kernels, body(): pl.pallas_call(kernel, out_shape=(out(TOK, 8 * REP * HD), out(2, 8, 2, TO...  82.7 us
    pallas_call x1, Pallas kernels, body(): pl.pallas_call(finish, out_shape=(jax.ShapeDtypeStruct(queries.shape, BF1...  2.52 us

profile of v1, /device:TPU:49, one launch (start us, length us, event | category | flops | bytes accessed | tf_op | source)
XLA Modules:
  0.0 85.9 jit_solution(11983306315689222862)
XLA Ops:
  0.6 82.7 %shard_map.119 = (bf16[32,8192]{1,0:T(8,128)(2,1)}, bf16[2,8,2,32,128]{4,3,2,1,0:T(8,128)(2,1)}, bf16[2,9,64,128]{3,2,1,0:T(8,128)(2,1)}) custom-call(bf16[32,8192]{1,0:T(8,128)(2,1)} %q_in.1, bf16[32,1024]{1,0:T(8,128)(2,1)} %k_in.1, bf16[32,1024]{1,0:T(8,128)(2,1)} %v_in.1, bf16[32,8192]{1,0:T(8,128)(2,1)} %g_in.1, bf16[64,128]{1,0:T(8,128)(2,1)} %pk_in.1, ...), custom_call_target="tpu_custom_call" | custom-call | flops 2000000000 | bytes 4000000 | tf_op jit(solution)/shard_map/pallas_call | solution.py:979
  83.3 2.5 %finish.1 = (bf16[32,8192]{1,0:T(8,128)(2,1)}, bf16[32,1024]{1,0:T(8,128)(2,1)}, bf16[32,1024]{1,0:T(8,128)(2,1)}, bf16[64,128]{1,0:T(8,128)(2,1)}, bf16[64,128]{1,0:T(8,128)(2,1)}) custom-call(bf16[32,8192]{1,0:T(8,128)(2,1)} %get-tuple-element.8.dq_in, bf16[2,8,2,32,128]{4,3,2,1,0:T(8,128)(2,1)} %get-tuple-element.9.dkvr_in, ...), custom_call_target="tpu_custom_call" | custom-call | tf_op jit(solution)/shard_map/finish/pallas_call | solution.py:1036

commit v2 on v1

--- a/solution.py
+++ b/solution.py
@@ -236,12 +236,7 @@
         for dy, dc in pairs:
             row_copy(dy, dc).start()
 
-    y_start((1, 0), (3, 0))
-
-    @pl.when(jnp.logical_not(own_core))
-    def _():
-        y_start((2, 0), (1, 1), (3, 1), (2, 1), (0, 1))
-
+    y_start((2, 0))
     own = pltpu.make_async_copy(side.at[head], rows.at[my_slot], r_ss.at[0])
     own.start()
 
@@ -382,14 +377,9 @@
                     x2_arrived(w, 0, s).wait_recv()
                     x2_arrived(w, 1, s).wait_recv()
 
-    def y_between(*pairs):
-        @pl.when(own_core)
-        def _():
-            y_start(*pairs)
-
     mine_wait(0)
     stop(0, 0)
-    y_between((2, 0), (1, 1), (3, 1))
+    y_start((1, 0))
     mine_wait(1)
     told(near_in)
     tell(far_in)
@@ -397,12 +387,14 @@
     stop(1, 0)
     told(far_in)
     rel_start(0)
-    y_between((2, 1), (0, 1))
+    y_start((2, 1), (3, 0))
     stop(0, 2)
     stop(1, 1)
     rel_pass(0)
     rel_start(1)
+    y_start((1, 1), (3, 1))
     last_arrivals(0)
+    y_start((0, 1))
     stop(1, 2)
     rel_pass(1)
     all_on(0, 0, LATE)
@@ -633,7 +625,6 @@
             dq = (dot_tn(kk[rho], ds_scr[i]) * SCALE).T.astype(BF16)
             for h in range(REP):
                 dqs[i, :, h * HD : (h + 1) * HD] = dq[h * TOK : (h + 1) * TOK]
-            send(dq_copy(i))
         return carry
 
     def part(w, x_, n, half):
@@ -796,6 +787,8 @@
         @pl.when(i >= 1)
         def _():
             second(0, order(i - 1))
+            send(dq_copy(2 * i - 2))
+            send(dq_copy(2 * i - 1))
 
         return carry
 

time: 86.1 us -> 84.9 us (0.986)
  the two profiles are of different devices: /device:TPU:49 before, /device:TPU:81 now
where the time goes in v2:
time: 84.9 us; the launch traced here: 84.6 us
  Pallas kernels  84 us (99%)
    pallas_call x1, Pallas kernels, body(): pl.pallas_call(kernel, out_shape=(out(TOK, 8 * REP * HD), out(2, 8, 2, TO...  81.5 us
    pallas_call x1, Pallas kernels, body(): pl.pallas_call(finish, out_shape=(jax.ShapeDtypeStruct(queries.shape, BF1...  2.52 us

profile of v2, /device:TPU:81, one launch (start us, length us, event | category | flops | bytes accessed | tf_op | source)
XLA Modules:
  0.0 84.6 jit_solution(10407713165737471186)
XLA Ops:
  0.6 81.5 %shard_map.119 = (bf16[32,8192]{1,0:T(8,128)(2,1)}, bf16[2,8,2,32,128]{4,3,2,1,0:T(8,128)(2,1)}, bf16[2,9,64,128]{3,2,1,0:T(8,128)(2,1)}) custom-call(bf16[32,8192]{1,0:T(8,128)(2,1)} %q_in.1, bf16[32,1024]{1,0:T(8,128)(2,1)} %k_in.1, bf16[32,1024]{1,0:T(8,128)(2,1)} %v_in.1, bf16[32,8192]{1,0:T(8,128)(2,1)} %g_in.1, bf16[64,128]{1,0:T(8,128)(2,1)} %pk_in.1, ...), custom_call_target="tpu_custom_call" | custom-call | flops 2000000000 | bytes 4000000 | tf_op jit(solution)/shard_map/pallas_call | solution.py:972
  82.1 2.5 %finish.1 = (bf16[32,8192]{1,0:T(8,128)(2,1)}, bf16[32,1024]{1,0:T(8,128)(2,1)}, bf16[32,1024]{1,0:T(8,128)(2,1)}, bf16[64,128]{1,0:T(8,128)(2,1)}, bf16[64,128]{1,0:T(8,128)(2,1)}) custom-call(bf16[32,8192]{1,0:T(8,128)(2,1)} %get-tuple-element.8.dq_in, bf16[2,8,2,32,128]{4,3,2,1,0:T(8,128)(2,1)} %get-tuple-element.9.dkvr_in, ...), custom_call_target="tpu_custom_call" | custom-call | tf_op jit(solution)/shard_map/finish/pallas_call | solution.py:1029

commit v3 on v2

--- a/solution.py
+++ b/solution.py
@@ -393,12 +393,14 @@
     rel_pass(0)
     rel_start(1)
     y_start((1, 1), (3, 1))
+    all_on(0, 0, 3)
     last_arrivals(0)
+    stop(1, 2)
+    all_on(0, 3, LATE)
     y_start((0, 1))
-    stop(1, 2)
     rel_pass(1)
-    all_on(0, 0, LATE)
     last_arrivals(1)
+    all_on(1, 0, 3)
 
     for dy, dc in far:
         ref = rows.at[slot_of(lax.rem(y + dy, Y), lax.rem(c + dc, C))]
@@ -572,10 +574,6 @@
 
         @pl.when(rho == 0)
         def _():
-            all_on(1, 0, 3)
-
-        @pl.when(rho == 1)
-        def _():
             all_on(1, 3, LATE)
 
         return carry
@@ -705,10 +703,10 @@
         rx_copy(w, 0, n).wait_recv()
         ra[w, n] = (ra[w, n].astype(F32) + own_part(w, xr, n, 0)).astype(BF16)
         rx2_copy(w, 0, n).start()
-        rx_copy(w, 2, n).start()
         rx_copy(w, 1, n).wait_recv()
         rb[w, n] = (rb[w, n].astype(F32) + own_part(w, xl, n, 1)).astype(BF16)
         rx2_copy(w, 1, n).start()
+        rx_copy(w, 2, n).start()
         rx_copy(w, 3, n).start()
 
     def second(w, n):
@@ -775,6 +773,8 @@
         @pl.when(i < 4)
         def _():
             first(0, order(i))
+            send(dq_copy(2 * i))
+            send(dq_copy(2 * i + 1))
 
         @pl.when(i == 1)
         def _():
@@ -787,8 +787,6 @@
         @pl.when(i >= 1)
         def _():
             second(0, order(i - 1))
-            send(dq_copy(2 * i - 2))
-            send(dq_copy(2 * i - 1))
 
         return carry
 

time: 84.9 us -> 84.7 us (level)
  no operation moved by 1% of the time
where the time goes in v3:
time: 84.7 us; the launch traced here: 84.4 us
  Pallas kernels  83.8 us (99%)
    pallas_call x1, Pallas kernels, body(): pl.pallas_call(kernel, out_shape=(out(TOK, 8 * REP * HD), out(2, 8, 2, TO...  81.3 us
    pallas_call x1, Pallas kernels, body(): pl.pallas_call(finish, out_shape=(jax.ShapeDtypeStruct(queries.shape, BF1...  2.52 us

profile of v3, /device:TPU:81, one launch (start us, length us, event | category | flops | bytes accessed | tf_op | source)
XLA Modules:
  0.0 84.4 jit_solution(1515043893640908088)
XLA Ops:
  0.6 81.3 %shard_map.119 = (bf16[32,8192]{1,0:T(8,128)(2,1)}, bf16[2,8,2,32,128]{4,3,2,1,0:T(8,128)(2,1)}, bf16[2,9,64,128]{3,2,1,0:T(8,128)(2,1)}) custom-call(bf16[32,8192]{1,0:T(8,128)(2,1)} %q_in.1, bf16[32,1024]{1,0:T(8,128)(2,1)} %k_in.1, bf16[32,1024]{1,0:T(8,128)(2,1)} %v_in.1, bf16[32,8192]{1,0:T(8,128)(2,1)} %g_in.1, bf16[64,128]{1,0:T(8,128)(2,1)} %pk_in.1, ...), custom_call_target="tpu_custom_call" | custom-call | flops 2000000000 | bytes 4000000 | tf_op jit(solution)/shard_map/pallas_call | solution.py:970
  81.9 2.5 %finish.1 = (bf16[32,8192]{1,0:T(8,128)(2,1)}, bf16[32,1024]{1,0:T(8,128)(2,1)}, bf16[32,1024]{1,0:T(8,128)(2,1)}, bf16[64,128]{1,0:T(8,128)(2,1)}, bf16[64,128]{1,0:T(8,128)(2,1)}) custom-call(bf16[32,8192]{1,0:T(8,128)(2,1)} %get-tuple-element.8.dq_in, bf16[2,8,2,32,128]{4,3,2,1,0:T(8,128)(2,1)} %get-tuple-element.9.dkvr_in, ...), custom_call_target="tpu_custom_call" | custom-call | tf_op jit(solution)/shard_map/finish/pallas_call | solution.py:1027

commit v4 on v3

--- a/solution.py
+++ b/solution.py
@@ -766,8 +766,6 @@
     spread_all(0)
     drel_pass(0, 0)
     lax.fori_loop(0, 4, query_grads, 0)
-    second(1, order(2))
-    second(1, order(3))
 
     def last(i, carry):
         @pl.when(i < 4)
@@ -775,6 +773,10 @@
             first(0, order(i))
             send(dq_copy(2 * i))
             send(dq_copy(2 * i + 1))
+
+        @pl.when(i < 2)
+        def _():
+            second(1, order(i + 2))
 
         @pl.when(i == 1)
         def _():

time: 84.7 us -> 85.2 us (level)
  the two profiles are of different devices: /device:TPU:81 before, /device:TPU:89 now
where the time goes in v4:
time: 85.2 us; the launch traced here: 85 us
  Pallas kernels  84.3 us (99%)
    pallas_call x1, Pallas kernels, body(): pl.pallas_call(kernel, out_shape=(out(TOK, 8 * REP * HD), out(2, 8, 2, TO...  81.8 us
    pallas_call x1, Pallas kernels, body(): pl.pallas_call(finish, out_shape=(jax.ShapeDtypeStruct(queries.shape, BF1...  2.52 us

profile of v4, /device:TPU:89, one launch (start us, length us, event | category | flops | bytes accessed | tf_op | source)
XLA Modules:
  0.0 85.0 jit_solution(11747830118616688567)
XLA Ops:
  0.6 81.8 %shard_map.119 = (bf16[32,8192]{1,0:T(8,128)(2,1)}, bf16[2,8,2,32,128]{4,3,2,1,0:T(8,128)(2,1)}, bf16[2,9,64,128]{3,2,1,0:T(8,128)(2,1)}) custom-call(bf16[32,8192]{1,0:T(8,128)(2,1)} %q_in.1, bf16[32,1024]{1,0:T(8,128)(2,1)} %k_in.1, bf16[32,1024]{1,0:T(8,128)(2,1)} %v_in.1, bf16[32,8192]{1,0:T(8,128)(2,1)} %g_in.1, bf16[64,128]{1,0:T(8,128)(2,1)} %pk_in.1, ...), custom_call_target="tpu_custom_call" | custom-call | flops 2000000000 | bytes 4000000 | tf_op jit(solution)/shard_map/pallas_call | solution.py:972
  82.5 2.5 %finish.1 = (bf16[32,8192]{1,0:T(8,128)(2,1)}, bf16[32,1024]{1,0:T(8,128)(2,1)}, bf16[32,1024]{1,0:T(8,128)(2,1)}, bf16[64,128]{1,0:T(8,128)(2,1)}, bf16[64,128]{1,0:T(8,128)(2,1)}) custom-call(bf16[32,8192]{1,0:T(8,128)(2,1)} %get-tuple-element.8.dq_in, bf16[2,8,2,32,128]{4,3,2,1,0:T(8,128)(2,1)} %get-tuple-element.9.dkvr_in, ...), custom_call_target="tpu_custom_call" | custom-call | tf_op jit(solution)/shard_map/finish/pallas_call | solution.py:1029
